TPU v7x, 32 devices: a whole 2x2x4 slice. The times are simulated.
32 devices in a mesh: section: 8 (over y, x, core), kv: 4 (over z).
Axes of the slice: x: 2, y: 2, z: 4, core: 2. Of those that a mesh axis runs over, the one named last changes fastest.
Arguments:
- query: bfloat16 [8, 512, 4096], P('section', None, 'kv'), parts along dimension 2, may hold values from -6 to 6
- grad_output: bfloat16 [8, 512, 4096], P('section', None, 'kv'), parts along dimension 2, may hold values from -150 to 150
- log_total: bfloat16 [8, 512, 32], P('section', None, 'kv'), parts along dimension 2, may hold values from -1 to 10, as said below
- offset: bfloat16 [8, 512, 32], P('section', None, 'kv'), parts along dimension 2, may hold values from -600 to 600
- slice_keys: bfloat16 [8, 512, 1024], P('section', None, 'kv'), parts along dimension 2, may hold values from -7 to 7
- pool_keys: bfloat16 [8, 1536, 1024], P('section', None, 'kv'), parts along dimension 2, may hold values from -7 to 7
- block_table: int32 [8, 3], P('section'), may hold values from 0 to 2, each once within a row
Outputs:
- query_grad: bfloat16 [8, 512, 4096], P('section', None, 'kv'), parts along dimension 2
- slice_grad: bfloat16 [8, 512, 1024], P('section', None, 'kv'), parts along dimension 2
- pool_grad: bfloat16 [8, 1536, 1024], P('section', None, 'kv'), parts along dimension 2
There are 4 independent parts, one for each index of `kv`. A program takes and returns all parts, laid end to end along the dimension named above; an argument that names none is the same for every part. Nothing has to cross between parts.
Inputs may be any that keep to these rules, and one draw needn't show every extreme that they name: Each row of block_table names every slot 0 to 2 once. log_total lies near the log of the count of visible keys of the row plus one half.
All inputs are finite; a program needn't handle non-finite values.
Results may differ from a plain program's by a relative error of at most 0.0051.
Values may be sent and summed in bfloat16 or wider, within the bound.
A program may use at most 128 MiB of HBM per device.

v0:
```python
import jax
import jax.numpy as jnp
from jax import lax
from jax.sharding import PartitionSpec as P

NSL = 4


def passed_along(x, axis, by):
    length = lax.axis_size(axis)
    return lax.ppermute(x, axis, [(i, (i + by) % length) for i in range(length)])


def block_terms(queries, out_grads, totals, offsets, key_data, value_data, causal):
    score_scale = key_data.shape[1] ** (-0.5)
    scores = (
        jnp.einsum("rhd,cd->rhc", queries, key_data, preferred_element_type=jnp.float32)
        * score_scale
    )
    weights = jnp.exp(scores - totals.astype(jnp.float32)[:, :, None])
    if causal:
        row_ids = jnp.arange(queries.shape[0], dtype=jnp.int32)
        visible = row_ids[:, None] >= row_ids[None, :]
        weights = jnp.where(visible[:, None, :], weights, jnp.zeros_like(weights))
    weight_grad = jnp.einsum(
        "rhd,cd->rhc", out_grads, value_data, preferred_element_type=jnp.float32
    )
    score_grad = weights * (weight_grad - offsets.astype(jnp.float32)[:, :, None])
    weights_low = weights.astype(jnp.bfloat16)
    score_low = score_grad.astype(jnp.bfloat16)
    query_part = (
        jnp.einsum("rhc,cd->rhd", score_low, key_data, preferred_element_type=jnp.float32)
        * score_scale
    )
    key_part = (
        jnp.einsum("rhc,rhd->cd", score_low, queries, preferred_element_type=jnp.float32)
        * score_scale
    )
    value_part = jnp.einsum(
        "rhc,rhd->cd", weights_low, out_grads, preferred_element_type=jnp.float32
    )
    return (query_part, jnp.concatenate([key_part, value_part], axis=1))


def pool_terms(queries, out_grads, totals, offsets, pool_block, slot_order, block_count):
    head_size = pool_block.shape[1] // 2
    slice_rows = queries.shape[0]
    query_sum = jnp.zeros(queries.shape, jnp.float32)
    pool_sum = jnp.zeros(pool_block.shape, jnp.float32)

    def add_block(position, carry):
        query_acc, grad_acc = carry
        row_start = slot_order[position] * slice_rows
        key_block = lax.dynamic_slice_in_dim(pool_block, row_start, slice_rows, 0)
        query_part, block_grad = block_terms(
            queries,
            out_grads,
            totals,
            offsets,
            key_block[:, :head_size],
            key_block[:, head_size:],
            False,
        )
        grad_acc = lax.dynamic_update_slice_in_dim(grad_acc, block_grad, row_start, 0)
        return (query_acc + query_part, grad_acc)

    return lax.fori_loop(0, block_count, add_block, (query_sum, pool_sum))


def per_device(query, grad_output, log_total, offset, slice_keys, pool_keys, block_table):
    slice_rows = slice_keys.shape[1]
    head_size = slice_keys.shape[2] // 2
    head_count = log_total.shape[2]
    queries = query[0].reshape(slice_rows, head_count, head_size)
    out_grads = grad_output[0].reshape(slice_rows, head_count, head_size)
    totals = log_total[0]
    offsets = offset[0]
    own_block = slice_keys[0]
    pool_block = pool_keys[0]
    slot_order = block_table[0]
    pool_slots = slot_order.shape[0]
    sections = lax.axis_size("section")
    half_axis = sections // 2
    group_size = sections // NSL
    layer_index = lax.axis_index("section")
    slice_depth = NSL - 1 - layer_index // group_size % (NSL - 1)
    own_query, own_grad = block_terms(
        queries,
        out_grads,
        totals,
        offsets,
        own_block[:, :head_size],
        own_block[:, head_size:],
        True,
    )
    ordered = jnp.concatenate(
        [
            lax.dynamic_slice_in_dim(pool_block, slot_order[position] * slice_rows, slice_rows, 0)
            for position in range(pool_slots)
        ],
        axis=0,
    )
    arrived = passed_along(ordered, "section", half_axis)
    straight = jnp.arange(pool_slots, dtype=jnp.int32)
    pool_query, ordered_grad = pool_terms(
        queries, out_grads, totals, offsets, arrived, straight, slice_depth
    )
    returned = passed_along(ordered_grad.astype(jnp.bfloat16), "section", -half_axis)
    query_sum = own_query + pool_query.astype(jnp.bfloat16).astype(jnp.float32)
    pool_sum = jnp.zeros(pool_block.shape, jnp.float32)
    for position in range(pool_slots):
        row_start = slot_order[position] * slice_rows
        incoming = lax.dynamic_slice_in_dim(returned, position * slice_rows, slice_rows, 0)
        pool_sum = lax.dynamic_update_slice_in_dim(
            pool_sum, incoming.astype(jnp.float32), row_start, 0
        )
    query_grad = query_sum.reshape(slice_rows, head_count * head_size).astype(jnp.bfloat16)[None]
    return (query_grad, own_grad.astype(jnp.bfloat16)[None], pool_sum.astype(jnp.bfloat16)[None])


def solution(mesh):
    return jax.shard_map(
        per_device,
        mesh=mesh,
        in_specs=(
            P("section", None, "kv"),
            P("section", None, "kv"),
            P("section", None, "kv"),
            P("section", None, "kv"),
            P("section", None, "kv"),
            P("section", None, "kv"),
            P("section", None),
        ),
        out_specs=(P("section", None, "kv"), P("section", None, "kv"), P("section", None, "kv")),
        check_vma=False,
    )
```

profile of v0, /device:TPU:0, one launch (start us, length us, event | category | flops | bytes accessed | tf_op | source)
XLA Modules:
  0.0 119.6 jit_solution(8495812560894490626)
XLA Ops:
  0.6 1.4 %fusion.33 = (s32[1,1]{1,0:T(1,128)}, s32[1,1]{1,0:T(1,128)}, s32[1,1]{1,0:T(1,128)}) fusion(s32[1,3]{1,0:T(1,128)} %param.15), kind=kLoop, calls=%fused_computation.49 | loop fusion | bytes 24 | tf_op jit(solution)/shard_map/slice | solution.py:98
  4.0 1.2 dynamic-slice_bitcast_fusion.7
  6.1 3.0 %collective-permute-start = (bf16[1536,256]{1,0:T(8,128)(2,1)}, bf16[1536,256]{1,0:T(8,128)(2,1)S(1)}, u32[]{:S(2)}, u32[]{:S(2)}) collective-permute-start(bf16[1536,256]{1,0:T(8,128)(2,1)} %pad_maximum_fusion.1), channel_id=1, source_target_pairs={{0,16},{4,20},{8,24},{12,28},{16,0},{20,4},{24,8},{28,12},{1,17},{... | collective-permute-start | bytes 2359304 | tf_op jit(solution)/shard_map/ppermute | solution.py:11
  9.1 1.5 %copy.17 = bf16[1,512,1024]{1,2,0:T(8,128)(2,1)S(1)} copy(bf16[1,512,1024]{2,1,0:T(8,128)(2,1)} %param.10) | data formatting | bytes 2097152 | tf_op args[1]
  10.6 1.9 %copy.15 = bf16[1,512,1024]{1,2,0:T(8,128)(2,1)S(1)} copy(bf16[1,512,1024]{2,1,0:T(8,128)(2,1)} %param.9) | data formatting | bytes 2097152 | tf_op args[0]
  12.5 1.3 %fusion.30 = f32[512,8,512]{2,0,1:T(8,128)S(1)} fusion(bf16[512,8,128]{0,2,1:T(8,128)(2,1)S(1)} %bitcast.107, bf16[512,256]{1,0:T(8,128)(2,1)S(1)} %bitcast.118), kind=kOutput, calls=%fused_computation.44 | convolution fusion | flops 536870912 | bytes 9568256 | tf_op jit(solution)/shard_map/rhd,cd->rhc/dot_general | solution.py:17
  14.5 3.5 %multiply_convert_fusion.1 = bf16[512,8,512]{2,0,1:T(8,128)(2,1)S(1)} fusion(f32[512,8,512]{2,0,1:T(8,128)S(1)} %fusion.30, f32[512,8]{0,1:T(8,128)S(1)} %get-tuple-element.98, f32[512,8]{0,1:T(8,128)S(1)} %get-tuple-element.99, pred[512,512]{1,0:T(8,128)(4,1)S(1)} %iota_compare_fusion, bf16[512,8,128]{0,2,1:T(8,128)(2,1)S(1)} %bitcast.110, ...), kind=kOutput, calls=%fused_computation.18 | convolution fusion | flops 549453824 | bytes 14057472 | tf_op jit(solution)/shard_map/rhd,cd->rhc/dot_general | solution.py:25
  18.0 2.0 %copy-done.4 = bf16[512,8,512]{2,0,1:T(8,128)(2,1)} copy-done((bf16[512,8,512]{2,0,1:T(8,128)(2,1)}, bf16[512,8,512]{2,0,1:T(8,128)(2,1)S(1)}, u32[]{:S(2)}) %copy-start.4) | copy-done | bytes 4194328
  20.8 5.2 %fusion.26 = bf16[1,512,128]{1,2,0:T(8,128)(2,1)} fusion(bf16[512,8,128]{0,2,1:T(8,128)(2,1)S(1)} %bitcast.111, f32[512,8,512]{2,0,1:T(8,128)} %copy-done.5, f32[512,8]{0,1:T(8,128)S(1)} %copy-done.12, pred[512,512]{1,0:T(8,128)(4,1)S(1)} %iota_compare_fusion), kind=kOutput, calls=%fused_computation.30 | convolution fusion | flops 545325056 | bytes 9846784 | tf_op jit(solution)/shard_map/rhc,rhd->cd/dot_general | solution.py:39
  28.7 67.9 %while.12 = (s32[]{:T(128)}, f32[512,8,128]{2,0,1:T(8,128)S(1)}, bf16[1536,256]{1,0:T(8,128)(2,1)}, s32[]{:T(128)}, s32[3]{0:T(128)S(1)}, /*index=5*/bf16[1536,2...) while((s32[]{:T(128)}, f32[512,8,128]{2,0,1:T(8,128)S(1)}, ...), condition=%wide.region_1.2_spmd, body=%wide.region_0.1_spmd.sunk | while | flops 2702843904 | bytes 102990344 | solution.py:67
  30.0 5.4 %fusion.64 = f32[512,512,8]{1,0,2:T(8,128)} fusion(bf16[512,8,128]{0,2,1:T(8,128)(2,1)S(1)} %get-tuple-element.200, bf16[1536,256]{1,0:T(8,128)(2,1)} %get-tuple-element.199, s32[]{:T(128)S(6)} %select_n.55), kind=kOutput, calls=%fused_computation.13.clone.1 | convolution fusion | flops 536870912 | bytes 9568260 | tf_op jit(solution)/shard_map/while/body/rhd,cd->rhc/dot_general | solution.py:17
  35.4 5.9 %fusion.65 = bf16[512,8,512]{0,2,1:T(8,128)(2,1)S(1)} fusion(f32[512,512,8]{1,0,2:T(8,128)} %fusion.64, f32[512,8]{0,1:T(8,128)S(1)} %convert_element_type.124, f32[512,8]{0,1:T(8,128)S(1)} %convert_element_type.125, bf16[512,8,128]{0,2,1:T(8,128)(2,1)} %get-tuple-element.202, bf16[1536,256]{1,0:T(8,128)(2,1)} %get-tuple-element.199, ...), kind=kOutput, calls=%fused_computation.4.clone.1 | convolution fusion | flops 547356672 | bytes 13795336 | tf_op jit(solution)/shard_map/while/body/rhd,cd->rhc/dot_general | solution.py:25
  41.3 1.4 %fusion.67 = bf16[512,128]{0,1:T(8,128)(2,1)S(1)} fusion(bf16[512,8,512]{0,2,1:T(8,128)(2,1)S(1)} %fusion.65, bf16[512,8,128]{0,2,1:T(8,128)(2,1)S(1)} %get-tuple-element.200), kind=kOutput, calls=%fused_computation.8.clone.1 | convolution fusion | flops 537001984 | bytes 5373952 | tf_op jit(solution)/shard_map/while/body/rhc,rhd->cd/dot_general | solution.py:36
  43.3 1.7 %fusion.66 = bf16[512,128]{0,1:T(8,128)(2,1)S(1)} fusion(bf16[512,8,128]{0,2,1:T(8,128)(2,1)S(1)} %copy-done.3, f32[512,512,8]{1,0,2:T(8,128)S(1)} %copy-done, f32[512,8]{0,1:T(8,128)S(1)} %convert_element_type.125), kind=kOutput, calls=%fused_computation.9.clone.1 | convolution fusion | flops 543162368 | bytes 9584640 | tf_op jit(solution)/shard_map/while/body/rhc,rhd->cd/dot_general | solution.py:39
  45.9 1.7 %constant_dynamic-update-slice_fusion.2 = bf16[1536,256]{1,0:T(8,128)(2,1)} fusion(bf16[1536,256]{1,0:T(8,128)(2,1)} %get-tuple-element.180, bf16[512,256]{1,0:T(8,128)(2,1)} %copy.37, s32[]{:T(128)S(6)} %select_n.55), kind=kLoop, calls=%fused_computation.16.clone.1 | loop fusion | bytes 524292 | tf_op jit(solution)/shard_map/while/body/dynamic_update_slice | solution.py:64
  47.6 3.8 %multiply_add_fusion.2 = f32[512,8,128]{2,0,1:T(8,128)S(1)} fusion(f32[512,8,128]{2,0,1:T(8,128)S(1)} %get-tuple-element.179, bf16[512,8,512]{0,2,1:T(8,128)(2,1)} %copy-done.1, bf16[1536,256]{1,0:T(8,128)(2,1)} %get-tuple-element.199, s32[]{:T(128)S(6)} %select_n.55), kind=kOutput, calls=%fused_computation.6.clone.1 | convolution fusion | flops 537919488 | bytes 8519684 | tf_op jit(solution)/shard_map/while/body/rhc,cd->rhd/dot_general | solution.py:32
  52.6 5.4 %fusion.64 = f32[512,512,8]{1,0,2:T(8,128)} fusion(bf16[512,8,128]{0,2,1:T(8,128)(2,1)S(1)} %get-tuple-element.200, bf16[1536,256]{1,0:T(8,128)(2,1)} %get-tuple-element.199, s32[]{:T(128)S(6)} %select_n.55), kind=kOutput, calls=%fused_computation.13.clone.1 | convolution fusion | flops 536870912 | bytes 9568260 | tf_op jit(solution)/shard_map/while/body/rhd,cd->rhc/dot_general | solution.py:17
  58.0 5.9 %fusion.65 = bf16[512,8,512]{0,2,1:T(8,128)(2,1)S(1)} fusion(f32[512,512,8]{1,0,2:T(8,128)} %fusion.64, f32[512,8]{0,1:T(8,128)S(1)} %convert_element_type.124, f32[512,8]{0,1:T(8,128)S(1)} %convert_element_type.125, bf16[512,8,128]{0,2,1:T(8,128)(2,1)} %get-tuple-element.202, bf16[1536,256]{1,0:T(8,128)(2,1)} %get-tuple-element.199, ...), kind=kOutput, calls=%fused_computation.4.clone.1 | convolution fusion | flops 547356672 | bytes 13795336 | tf_op jit(solution)/shard_map/while/body/rhd,cd->rhc/dot_general | solution.py:25
  63.9 1.4 %fusion.67 = bf16[512,128]{0,1:T(8,128)(2,1)S(1)} fusion(bf16[512,8,512]{0,2,1:T(8,128)(2,1)S(1)} %fusion.65, bf16[512,8,128]{0,2,1:T(8,128)(2,1)S(1)} %get-tuple-element.200), kind=kOutput, calls=%fused_computation.8.clone.1 | convolution fusion | flops 537001984 | bytes 5373952 | tf_op jit(solution)/shard_map/while/body/rhc,rhd->cd/dot_general | solution.py:36
  65.9 1.7 %fusion.66 = bf16[512,128]{0,1:T(8,128)(2,1)S(1)} fusion(bf16[512,8,128]{0,2,1:T(8,128)(2,1)S(1)} %copy-done.3, f32[512,512,8]{1,0,2:T(8,128)S(1)} %copy-done, f32[512,8]{0,1:T(8,128)S(1)} %convert_element_type.125), kind=kOutput, calls=%fused_computation.9.clone.1 | convolution fusion | flops 543162368 | bytes 9584640 | tf_op jit(solution)/shard_map/while/body/rhc,rhd->cd/dot_general | solution.py:39
  68.5 1.7 %constant_dynamic-update-slice_fusion.2 = bf16[1536,256]{1,0:T(8,128)(2,1)} fusion(bf16[1536,256]{1,0:T(8,128)(2,1)} %get-tuple-element.180, bf16[512,256]{1,0:T(8,128)(2,1)} %copy.37, s32[]{:T(128)S(6)} %select_n.55), kind=kLoop, calls=%fused_computation.16.clone.1 | loop fusion | bytes 524292 | tf_op jit(solution)/shard_map/while/body/dynamic_update_slice | solution.py:64
  70.2 3.8 %multiply_add_fusion.2 = f32[512,8,128]{2,0,1:T(8,128)S(1)} fusion(f32[512,8,128]{2,0,1:T(8,128)S(1)} %get-tuple-element.179, bf16[512,8,512]{0,2,1:T(8,128)(2,1)} %copy-done.1, bf16[1536,256]{1,0:T(8,128)(2,1)} %get-tuple-element.199, s32[]{:T(128)S(6)} %select_n.55), kind=kOutput, calls=%fused_computation.6.clone.1 | convolution fusion | flops 537919488 | bytes 8519684 | tf_op jit(solution)/shard_map/while/body/rhc,cd->rhd/dot_general | solution.py:32
  75.3 5.4 %fusion.64 = f32[512,512,8]{1,0,2:T(8,128)} fusion(bf16[512,8,128]{0,2,1:T(8,128)(2,1)S(1)} %get-tuple-element.200, bf16[1536,256]{1,0:T(8,128)(2,1)} %get-tuple-element.199, s32[]{:T(128)S(6)} %select_n.55), kind=kOutput, calls=%fused_computation.13.clone.1 | convolution fusion | flops 536870912 | bytes 9568260 | tf_op jit(solution)/shard_map/while/body/rhd,cd->rhc/dot_general | solution.py:17
  80.7 5.9 %fusion.65 = bf16[512,8,512]{0,2,1:T(8,128)(2,1)S(1)} fusion(f32[512,512,8]{1,0,2:T(8,128)} %fusion.64, f32[512,8]{0,1:T(8,128)S(1)} %convert_element_type.124, f32[512,8]{0,1:T(8,128)S(1)} %convert_element_type.125, bf16[512,8,128]{0,2,1:T(8,128)(2,1)} %get-tuple-element.202, bf16[1536,256]{1,0:T(8,128)(2,1)} %get-tuple-element.199, ...), kind=kOutput, calls=%fused_computation.4.clone.1 | convolution fusion | flops 547356672 | bytes 13795336 | tf_op jit(solution)/shard_map/while/body/rhd,cd->rhc/dot_general | solution.py:25
  86.6 1.4 %fusion.67 = bf16[512,128]{0,1:T(8,128)(2,1)S(1)} fusion(bf16[512,8,512]{0,2,1:T(8,128)(2,1)S(1)} %fusion.65, bf16[512,8,128]{0,2,1:T(8,128)(2,1)S(1)} %get-tuple-element.200), kind=kOutput, calls=%fused_computation.8.clone.1 | convolution fusion | flops 537001984 | bytes 5373952 | tf_op jit(solution)/shard_map/while/body/rhc,rhd->cd/dot_general | solution.py:36
  88.6 1.7 %fusion.66 = bf16[512,128]{0,1:T(8,128)(2,1)S(1)} fusion(bf16[512,8,128]{0,2,1:T(8,128)(2,1)S(1)} %copy-done.3, f32[512,512,8]{1,0,2:T(8,128)S(1)} %copy-done, f32[512,8]{0,1:T(8,128)S(1)} %convert_element_type.125), kind=kOutput, calls=%fused_computation.9.clone.1 | convolution fusion | flops 543162368 | bytes 9584640 | tf_op jit(solution)/shard_map/while/body/rhc,rhd->cd/dot_general | solution.py:39
  91.2 1.7 %constant_dynamic-update-slice_fusion.2 = bf16[1536,256]{1,0:T(8,128)(2,1)} fusion(bf16[1536,256]{1,0:T(8,128)(2,1)} %get-tuple-element.180, bf16[512,256]{1,0:T(8,128)(2,1)} %copy.37, s32[]{:T(128)S(6)} %select_n.55), kind=kLoop, calls=%fused_computation.16.clone.1 | loop fusion | bytes 524292 | tf_op jit(solution)/shard_map/while/body/dynamic_update_slice | solution.py:64
  92.8 3.8 %multiply_add_fusion.2 = f32[512,8,128]{2,0,1:T(8,128)S(1)} fusion(f32[512,8,128]{2,0,1:T(8,128)S(1)} %get-tuple-element.179, bf16[512,8,512]{0,2,1:T(8,128)(2,1)} %copy-done.1, bf16[1536,256]{1,0:T(8,128)(2,1)} %get-tuple-element.199, s32[]{:T(128)S(6)} %select_n.55), kind=kOutput, calls=%fused_computation.6.clone.1 | convolution fusion | flops 537919488 | bytes 8519684 | tf_op jit(solution)/shard_map/while/body/rhc,cd->rhd/dot_general | solution.py:32
  98.5 5.0 %fusion.29 = f32[512,8,128]{0,2,1:T(8,128)} fusion(bf16[512,8,512]{2,0,1:T(8,128)(2,1)} %copy-done.4, bf16[512,256]{1,0:T(8,128)(2,1)} %bitcast.117), kind=kOutput, calls=%fused_computation.43 | convolution fusion | flops 536870912 | bytes 6422528 | tf_op jit(solution)/shard_map/rhc,cd->rhd/dot_general | solution.py:32
  104.1 1.9 %add_convert_fusion = bf16[512,8,128]{0,2,1:T(8,128)(2,1)S(1)} fusion(f32[512,8,128]{0,2,1:T(8,128)} %fusion.29, bf16[512,8,128]{0,2,1:T(8,128)(2,1)S(1)} %copy.21), kind=kLoop, calls=%fused_computation.23 | loop fusion | flops 2097152 | bytes 4194304 | tf_op jit(solution)/shard_map/convert_element_type | solution.py:117
  106.1 1.3 %copy.23 = bf16[1,512,1024]{2,1,0:T(8,128)(2,1)} copy(bf16[1,512,1024]{1,2,0:T(8,128)(2,1)S(1)} %bitcast.113) | data formatting | bytes 2097152
  107.4 8.4 %collective-permute-done.1 = bf16[1536,256]{1,0:T(8,128)(2,1)} collective-permute-done((bf16[1536,256]{1,0:T(8,128)(2,1)}, bf16[1536,256]{1,0:T(8,128)(2,1)}, u32[]{:S(2)}, u32[]{:S(2)}) %collective-permute-start.1) | collective-permute-done | bytes 786464 | tf_op jit(solution)/shard_map/ppermute | solution.py:11
  (80 shorter events, 17.4 us)
Async XLA Ops:
  0.6 11.9 %copy-start.10 = (bf16[1,512,256]{2,1,0:T(8,128)(2,1)S(1)}, bf16[1,512,256]{2,1,0:T(8,128)(2,1)}, u32[]{:S(2)}) copy-start(bf16[1,512,256]{2,1,0:T(8,128)(2,1)} %param.13) | copy-start | bytes 786436
  6.1 20.7 %collective-permute-start = (bf16[1536,256]{1,0:T(8,128)(2,1)}, bf16[1536,256]{1,0:T(8,128)(2,1)S(1)}, u32[]{:S(2)}, u32[]{:S(2)}) collective-permute-start(bf16[1536,256]{1,0:T(8,128)(2,1)} %pad_maximum_fusion.1), channel_id=1, source_target_pairs={{0,16},{4,20},{8,24},{12,28},{16,0},{20,4},{24,8},{28,12},{1,17},{... | collective-permute-start | bytes 2359304 | tf_op jit(solution)/shard_map/ppermute | solution.py:11
  10.6 10.1 %copy-start.2 = (bf16[1,512,1024]{1,2,0:T(8,128)(2,1)}, bf16[1,512,1024]{1,2,0:T(8,128)(2,1)S(1)}, u32[]{:S(2)}) copy-start(bf16[1,512,1024]{1,2,0:T(8,128)(2,1)S(1)} %copy.17) | copy-start | bytes 3145732
  12.5 1.3 %copy-start.8 = (bf16[1,512,8]{1,2,0:T(8,128)(2,1)S(1)}, bf16[1,512,8]{1,2,0:T(8,128)(2,1)}, u32[]{:S(2)}) copy-start(bf16[1,512,8]{1,2,0:T(8,128)(2,1)} %param.12) | copy-start | bytes 24580
  12.5 1.3 %copy-start.9 = (bf16[1,512,8]{1,2,0:T(8,128)(2,1)S(1)}, bf16[1,512,8]{1,2,0:T(8,128)(2,1)}, u32[]{:S(2)}) copy-start(bf16[1,512,8]{1,2,0:T(8,128)(2,1)} %param.11) | copy-start | bytes 24580
  13.8 4.2 %copy-start.5 = (f32[512,8,512]{2,0,1:T(8,128)}, f32[512,8,512]{2,0,1:T(8,128)S(1)}, u32[]{:S(2)}) copy-start(f32[512,8,512]{2,0,1:T(8,128)S(1)} %fusion.30) | copy-start | bytes 25165828
  13.9 0.7 copy-start.11
  18.0 2.0 %copy-start.4 = (bf16[512,8,512]{2,0,1:T(8,128)(2,1)}, bf16[512,8,512]{2,0,1:T(8,128)(2,1)S(1)}, u32[]{:S(2)}) copy-start(bf16[512,8,512]{2,0,1:T(8,128)(2,1)S(1)} %multiply_convert_fusion.1) | copy-start | bytes 12582916
  20.0 0.8 copy-start.12
  26.8 0.9 copy-start.6
  28.7 6.6 %copy-start.13 = (s32[3]{0:T(128)}, s32[3]{0:T(128)S(1)}, u32[]{:S(2)}) copy-start(s32[3]{0:T(128)S(1)} %get-tuple-element.198) | copy-start | bytes 40 | tf_op jit(solution)/shard_map/while
  35.4 7.4 %copy-start = (f32[512,512,8]{1,0,2:T(8,128)S(1)}, f32[512,512,8]{1,0,2:T(8,128)}, u32[]{:S(2)}) copy-start(f32[512,512,8]{1,0,2:T(8,128)} %fusion.64) | copy-start | bytes 25165828 | tf_op jit(solution)/shard_map/while
  41.3 3.7 %copy-start.1 = (bf16[512,8,512]{0,2,1:T(8,128)(2,1)}, bf16[512,8,512]{0,2,1:T(8,128)(2,1)S(1)}, u32[]{:S(2)}) copy-start(bf16[512,8,512]{0,2,1:T(8,128)(2,1)S(1)} %fusion.65) | copy-start | bytes 12582916 | tf_op jit(solution)/shard_map/while
  41.3 2.0 %copy-start.3 = (bf16[512,8,128]{0,2,1:T(8,128)(2,1)S(1)}, bf16[512,8,128]{0,2,1:T(8,128)(2,1)}, u32[]{:S(2)}) copy-start(bf16[512,8,128]{0,2,1:T(8,128)(2,1)} %get-tuple-element.202) | copy-start | bytes 3145732 | tf_op jit(solution)/shard_map/while
  47.6 3.8 %copy-start.14 = (s32[3]{0:T(128)S(1)}, s32[3]{0:T(128)}, u32[]{:S(2)}) copy-start(s32[3]{0:T(128)} %copy-done.13) | copy-start | bytes 40 | tf_op jit(solution)/shard_map/while
  51.4 6.6 %copy-start.13 = (s32[3]{0:T(128)}, s32[3]{0:T(128)S(1)}, u32[]{:S(2)}) copy-start(s32[3]{0:T(128)S(1)} %get-tuple-element.198) | copy-start | bytes 40 | tf_op jit(solution)/shard_map/while
  58.0 7.4 %copy-start = (f32[512,512,8]{1,0,2:T(8,128)S(1)}, f32[512,512,8]{1,0,2:T(8,128)}, u32[]{:S(2)}) copy-start(f32[512,512,8]{1,0,2:T(8,128)} %fusion.64) | copy-start | bytes 25165828 | tf_op jit(solution)/shard_map/while
  63.9 3.7 %copy-start.1 = (bf16[512,8,512]{0,2,1:T(8,128)(2,1)}, bf16[512,8,512]{0,2,1:T(8,128)(2,1)S(1)}, u32[]{:S(2)}) copy-start(bf16[512,8,512]{0,2,1:T(8,128)(2,1)S(1)} %fusion.65) | copy-start | bytes 12582916 | tf_op jit(solution)/shard_map/while
  63.9 2.0 %copy-start.3 = (bf16[512,8,128]{0,2,1:T(8,128)(2,1)S(1)}, bf16[512,8,128]{0,2,1:T(8,128)(2,1)}, u32[]{:S(2)}) copy-start(bf16[512,8,128]{0,2,1:T(8,128)(2,1)} %get-tuple-element.202) | copy-start | bytes 3145732 | tf_op jit(solution)/shard_map/while
  70.2 3.8 %copy-start.14 = (s32[3]{0:T(128)S(1)}, s32[3]{0:T(128)}, u32[]{:S(2)}) copy-start(s32[3]{0:T(128)} %copy-done.13) | copy-start | bytes 40 | tf_op jit(solution)/shard_map/while
  74.0 6.6 %copy-start.13 = (s32[3]{0:T(128)}, s32[3]{0:T(128)S(1)}, u32[]{:S(2)}) copy-start(s32[3]{0:T(128)S(1)} %get-tuple-element.198) | copy-start | bytes 40 | tf_op jit(solution)/shard_map/while
  80.7 7.4 %copy-start = (f32[512,512,8]{1,0,2:T(8,128)S(1)}, f32[512,512,8]{1,0,2:T(8,128)}, u32[]{:S(2)}) copy-start(f32[512,512,8]{1,0,2:T(8,128)} %fusion.64) | copy-start | bytes 25165828 | tf_op jit(solution)/shard_map/while
  86.6 3.7 %copy-start.1 = (bf16[512,8,512]{0,2,1:T(8,128)(2,1)}, bf16[512,8,512]{0,2,1:T(8,128)(2,1)S(1)}, u32[]{:S(2)}) copy-start(bf16[512,8,512]{0,2,1:T(8,128)(2,1)S(1)} %fusion.65) | copy-start | bytes 12582916 | tf_op jit(solution)/shard_map/while
  86.6 2.0 %copy-start.3 = (bf16[512,8,128]{0,2,1:T(8,128)(2,1)S(1)}, bf16[512,8,128]{0,2,1:T(8,128)(2,1)}, u32[]{:S(2)}) copy-start(bf16[512,8,128]{0,2,1:T(8,128)(2,1)} %get-tuple-element.202) | copy-start | bytes 3145732 | tf_op jit(solution)/shard_map/while
  92.8 3.8 %copy-start.14 = (s32[3]{0:T(128)S(1)}, s32[3]{0:T(128)}, u32[]{:S(2)}) copy-start(s32[3]{0:T(128)} %copy-done.13) | copy-start | bytes 40 | tf_op jit(solution)/shard_map/while
  96.6 19.1 %collective-permute-start.1 = (bf16[1536,256]{1,0:T(8,128)(2,1)}, bf16[1536,256]{1,0:T(8,128)(2,1)}, u32[]{:S(2)}, u32[]{:S(2)}) collective-permute-start(bf16[1536,256]{1,0:T(8,128)(2,1)} %get-tuple-element.58), channel_id=1, source_target_pairs={{0,16},{4,20},{8,24},{12,28},{16,0},{20,4},{24,8},{28,12},{1,17},{... | collective-permute-start | bytes 2359304 | tf_op jit(solution)/shard_map/ppermute | solution.py:11
  118.7 0.9 copy-start.7
where the time goes:
time: 120 us
  matrix products  70.3 us (59%)
  local copies, waits for them, and re-layouts  25.1 us (21%)
  waiting for transfers between devices  9.15 us (8%)
  other arithmetic  6.89 us (6%)
  starting transfers between devices  3.04 us (3%)
  between operations  2.83 us (2%)
  loops' own time  2.31 us (2%)
    dot_general x4, matrix products, block_terms(): jnp.einsum('rhd,cd->rhc', out_grads, value_data, preferred_element_type=j...  21.2 us
    dot_general x4, matrix products, block_terms(): jnp.einsum('rhd,cd->rhc', queries, key_data, preferred_element_type=jnp.f...  17.4 us
    dot_general x4, matrix products, block_terms(): jnp.einsum('rhc,cd->rhd', score_low, key_data, preferred_element_type=jnp...  16.3 us
    dot_general x4, matrix products, block_terms(): jnp.einsum('rhc,rhd->cd', weights_low, out_grads, preferred_element_type=...  10.3 us
    unnamed x24, local copies, waits for them, and re-layouts  9.94 us
    ppermute x2, waiting for transfers between devices, passed_along(): lax.ppermute(x, axis, [(i, (i + by) % length) for i in range(length)])  9.15 us
    dynamic_update_slice x6, local copies, waits for them, and re-layouts, add_block(): lax.dynamic_update_slice_in_dim(grad_acc, block_grad, row_start, 0)  7.53 us
    dot_general x4, matrix products, block_terms(): jnp.einsum('rhc,rhd->cd', score_low, queries, preferred_element_type=jnp....  5.04 us
  transfers between devices with their start and end apart: 2, of which 2 were waited for; matrix products, arithmetic and copies ran while one was open for 21% of the time, Pallas kernels for 0%

commit v1 on v0

v1 whole, which is shorter than its diff:
```python
import functools
import math

import jax
import jax.numpy as jnp
from jax import lax
from jax.experimental import pallas as pl
from jax.experimental.pallas import tpu as pltpu
from jax.sharding import PartitionSpec as P

PARTS = 1
LOG2E = math.log2(math.e)


def dot(a, b, ca, cb):
    return lax.dot_general(
        a, b, (((ca,), (cb,)), ((), ())), preferred_element_type=jnp.float32
    )


def kernel(
    slots, heads, table, q_hbm, g_hbm, lt_hbm, off_hbm, own_hbm, pool_hbm,
    dq_hbm, down_hbm, dpool_hbm,
    q, g, lt, off, own, pool, staged, arrived, outgoing, returned,
    dq, dq_low, dk, dv, down, dpool, lt_t, off_t,
    in_sem, out_sem, ksend, krecv, gsend, grecv,
):
    chunk = staged.shape[1]
    parts = staged.shape[0] // slots
    rows = q.shape[0]
    head = own.shape[1] // 2
    half = rows // 2
    scale = head ** (-0.5)
    sections = lax.axis_size("section")
    group = sections // (slots + 1)
    me = lax.axis_index("section")
    partner = lax.rem(me + sections // 2, sections)

    def chunks_of(layer):
        return parts * (slots - lax.rem(lax.div(layer, group), slots))

    mine, theirs = chunks_of(me), chunks_of(partner)

    ins = [
        pltpu.make_async_copy(src, dst, in_sem.at[n])
        for n, (src, dst) in enumerate(
            [(pool_hbm, pool), (own_hbm, own), (q_hbm, q), (g_hbm, g), (lt_hbm, lt), (off_hbm, off)]
        )
    ]
    for copy in ins:
        copy.start()
    barrier = pltpu.get_barrier_semaphore()
    pl.semaphore_signal(
        barrier, inc=1, device_id={"section": partner}, device_id_type=pl.DeviceIdType.MESH
    )
    ins[0].wait()
    for position in range(slots):
        for part in range(parts):
            staged[position * parts + part] = pool[table[0, position] * parts + part]
    pl.semaphore_wait(barrier, 1)

    def remote(src, dst, ssem, rsem, n):
        return pltpu.make_async_remote_copy(
            src_ref=src.at[n],
            dst_ref=dst.at[n],
            send_sem=ssem.at[n],
            recv_sem=rsem.at[n],
            device_id={"section": partner},
            device_id_type=pl.DeviceIdType.MESH,
        )

    def keys_copy(n):
        return remote(staged, arrived, ksend, krecv, n)

    def grads_copy(n):
        return remote(outgoing, returned, gsend, grecv, n)

    @pl.loop(0, theirs)
    def _(n):
        keys_copy(n).start()

    @pl.loop(theirs, slots * parts)
    def _(n):
        returned[n] = jnp.zeros(returned.shape[1:], returned.dtype)

    for copy in ins[1:]:
        copy.wait()
    lt_t[...] = lt[...].astype(jnp.float32) * LOG2E
    off_t[...] = off[...].astype(jnp.float32)

    def tile(key, value, h, first, mask):
        cols = slice(h * head, (h + 1) * head)
        qh = q[first:, cols]
        gh = g[first:, cols]
        scores = dot(key, qh, 1, 1)
        weights = jnp.exp2(scores * (scale * LOG2E) - lt_t[h : h + 1, first:])
        if mask is not None:
            weights = jnp.where(mask, weights, 0.0)
        grads = weights * (dot(value, gh, 1, 1) - off_t[h : h + 1, first:])
        weights_low = weights.astype(jnp.bfloat16)
        score_low = grads.astype(jnp.bfloat16)
        return (
            dot(score_low, key, 0, 0),
            dot(score_low, qh, 1, 0),
            dot(weights_low, gh, 1, 0),
        )

    for h in range(heads):
        cols = slice(h * head, (h + 1) * head)
        for t in range(2):
            first = t * half
            keys = slice(first, first + half)
            shape = (half, rows - first)
            mask = lax.broadcasted_iota(jnp.int32, shape, 1) >= lax.broadcasted_iota(
                jnp.int32, shape, 0
            )
            dq_t, dk_t, dv_t = tile(own[keys, :head], own[keys, head:], h, first, mask)
            if t == 0:
                dq[:, cols] = dq_t
            else:
                dq[first:, cols] += dq_t
            if h == 0:
                dk[keys] = dk_t
                dv[keys] = dv_t
            else:
                dk[keys] += dk_t
                dv[keys] += dv_t
    down[:, :head] = (dk[...] * scale).astype(down.dtype)
    down[:, head:] = dv[...].astype(down.dtype)
    down_out = pltpu.make_async_copy(down, down_hbm, out_sem.at[0])
    down_out.start()

    @pl.loop(0, mine)
    def _(n):
        keys_copy(n).wait_recv()
        for h in range(heads):
            cols = slice(h * head, (h + 1) * head)
            dq_t, dk_t, dv_t = tile(arrived[n, :, :head], arrived[n, :, head:], h, 0, None)
            dq[:, cols] += dq_t
            if h == 0:
                dk[:chunk] = dk_t
                dv[:chunk] = dv_t
            else:
                dk[:chunk] += dk_t
                dv[:chunk] += dv_t
        outgoing[n, :, :head] = (dk[:chunk] * scale).astype(outgoing.dtype)
        outgoing[n, :, head:] = dv[:chunk].astype(outgoing.dtype)
        grads_copy(n).start()

    dq_low[...] = (dq[...] * scale).astype(dq_low.dtype)
    dq_out = pltpu.make_async_copy(dq_low, dq_hbm, out_sem.at[1])
    dq_out.start()

    @pl.loop(0, theirs)
    def _(n):
        keys_copy(n).wait_send()
        grads_copy(n).wait_recv()

    for slot in range(slots):
        place = jnp.int32(0)
        for position in range(1, slots):
            place = jnp.where(table[0, position] == slot, position, place)
        for part in range(parts):
            dpool[slot * parts + part] = returned[place * parts + part]
    dpool_out = pltpu.make_async_copy(dpool, dpool_hbm, out_sem.at[2])
    dpool_out.start()

    @pl.loop(0, mine)
    def _(n):
        grads_copy(n).wait_send()

    down_out.wait()
    dq_out.wait()
    dpool_out.wait()


def per_device(query, grad_output, log_total, offset, slice_keys, pool_keys, block_table):
    rows, width = slice_keys.shape[1:]
    heads = log_total.shape[2]
    slots = block_table.shape[1]
    total = slots * PARTS
    chunk = rows // PARTS
    pool = pool_keys.reshape(total, chunk, width)
    low = jnp.bfloat16
    hbm = pl.BlockSpec(memory_space=pl.ANY)
    block = (total, chunk, width)
    dq, down, dpool = pl.pallas_call(
        functools.partial(kernel, slots, heads),
        out_shape=(
            jax.ShapeDtypeStruct(query.shape[1:], low),
            jax.ShapeDtypeStruct(slice_keys.shape[1:], low),
            jax.ShapeDtypeStruct(block, low),
        ),
        in_specs=[pl.BlockSpec(memory_space=pltpu.SMEM)] + [hbm] * 6,
        out_specs=(hbm, hbm, hbm),
        scratch_shapes=[
            pltpu.VMEM(query.shape[1:], low),
            pltpu.VMEM(query.shape[1:], low),
            pltpu.VMEM((heads, rows), low),
            pltpu.VMEM((heads, rows), low),
            pltpu.VMEM((rows, width), low),
            pltpu.VMEM(block, low),
            pltpu.VMEM(block, low),
            pltpu.VMEM(block, low),
            pltpu.VMEM(block, low),
            pltpu.VMEM(block, low),
            pltpu.VMEM(query.shape[1:], jnp.float32),
            pltpu.VMEM(query.shape[1:], low),
            pltpu.VMEM((rows, width // 2), jnp.float32),
            pltpu.VMEM((rows, width // 2), jnp.float32),
            pltpu.VMEM((rows, width), low),
            pltpu.VMEM(block, low),
            pltpu.VMEM((heads, rows), jnp.float32),
            pltpu.VMEM((heads, rows), jnp.float32),
            pltpu.SemaphoreType.DMA((6,)),
            pltpu.SemaphoreType.DMA((3,)),
            pltpu.SemaphoreType.DMA((total,)),
            pltpu.SemaphoreType.DMA((total,)),
            pltpu.SemaphoreType.DMA((total,)),
            pltpu.SemaphoreType.DMA((total,)),
        ],
        compiler_params=pltpu.CompilerParams(
            collective_id=0, has_side_effects=True, vmem_limit_bytes=48 * 1024 * 1024
        ),
        name="grads",
    )(block_table, query[0], grad_output[0], log_total[0].T, offset[0].T, slice_keys[0], pool)
    return dq[None], down[None], dpool.reshape(pool_keys.shape)


def solution(mesh):
    lanes = P("section", None, "kv")
    return jax.shard_map(
        per_device,
        mesh=mesh,
        in_specs=(lanes,) * 6 + (P("section", None),),
        out_specs=(lanes,) * 3,
        check_vma=False,
    )
```

time: 120 us -> 45.9 us (0.38)
  matrix products: 70.3 us -> 0 us
  Pallas kernels: 0 us -> 36.4 us
  local copies, waits for them, and re-layouts: 25.1 us -> 8.47 us
  waiting for transfers between devices: 9.15 us -> 0 us
  other arithmetic: 6.89 us -> 0 us
  starting transfers between devices: 3.04 us -> 0 us
  loops' own time: 2.31 us -> 0 us
  between operations: 2.83 us -> 0.66 us
    dot_general x20 -> x0, matrix products: 70.3 us -> none  [the longest x4 21.2 us: block_terms(): jnp.einsum('rhd,cd->rhc', out_grads, value_data, preferred_element_type=j...]
    pallas_call x0 -> x1, Pallas kernels: none -> 36.4 us  [per_device(): pl.pallas_call(functools.partial(kernel, slots, heads), out_shape=(jax.Sh...]
    ppermute x2 -> x0, waiting for transfers between devices: 9.15 us -> none  [passed_along(): lax.ppermute(x, axis, [(i, (i + by) % length) for i in range(length)])]
    dynamic_update_slice x6 -> x0, local copies, waits for them, and re-layouts: 7.53 us -> none  [add_block(): lax.dynamic_update_slice_in_dim(grad_acc, block_grad, row_start, 0)]
    ppermute x2 -> x0, starting transfers between devices: 3.04 us -> none  [passed_along(): lax.ppermute(x, axis, [(i, (i + by) % length) for i in range(length)])]
    dynamic_update_slice x3 -> x0, other arithmetic: 2.93 us -> none  [per_device(): lax.dynamic_update_slice_in_dim(pool_sum, incoming.astype(jnp.float32), r...]
    dynamic_slice x4 -> x0, local copies, waits for them, and re-layouts: 2.92 us -> none  [the longest x3 1.76 us: add_block(): row_start = slot_order[position] * slice_rows]
    another operation x1 -> x0, loops' own time: 2.31 us -> none  [pool_terms(): return lax.fori_loop(0, block_count, add_block, (query_sum, pool_sum))]
  transfers between devices with their start and end apart: 2 -> 0, of which waited for: 2 -> 0; matrix products, arithmetic and copies ran while one was open for 21% -> 0% of each run, Pallas kernels for 0% -> 0%
where the time goes in v1:
time: 45.9 us; the launch traced here: 45.5 us
  Pallas kernels  36.4 us (79%)
  local copies, waits for them, and re-layouts  8.47 us (18%)
  between operations  0.66 us (1%)
    pallas_call x1, Pallas kernels, per_device(): pl.pallas_call(functools.partial(kernel, slots, heads), out_shape=(jax.Sh...  36.4 us
    unnamed x17, local copies, waits for them, and re-layouts  8.47 us

profile of v1, /device:TPU:0, one launch (start us, length us, event | category | flops | bytes accessed | tf_op | source)
XLA Modules:
  0.0 45.5 jit_solution(18102561027947145372)
XLA Ops:
  0.6 0.0 copy-start.4
  0.6 0.0 copy-start.6
  0.7 0.7 %copy-done.4 = bf16[1,512,8]{1,2,0:T(8,128)(2,1)S(1)} copy-done((bf16[1,512,8]{1,2,0:T(8,128)(2,1)S(1)}, bf16[1,512,8]{1,2,0:T(8,128)(2,1)}, u32[]{:S(2)}) %copy-start.4) | copy-done | bytes 8216
  1.3 0.0 copy-done.6
  1.3 0.0 copy-start
  1.3 1.2 %copy-done = bf16[1,512,1024]{2,1,0:T(8,128)(2,1)S(1)} copy-done((bf16[1,512,1024]{2,1,0:T(8,128)(2,1)S(1)}, bf16[1,512,1024]{2,1,0:T(8,128)(2,1)}, u32[]{:S(2)}) %copy-start) | copy-done | bytes 1048600
  2.6 0.0 copy-start.1
  2.6 1.2 %copy-done.1 = bf16[1,512,1024]{2,1,0:T(8,128)(2,1)S(1)} copy-done((bf16[1,512,1024]{2,1,0:T(8,128)(2,1)S(1)}, bf16[1,512,1024]{2,1,0:T(8,128)(2,1)}, u32[]{:S(2)}) %copy-start.1) | copy-done | bytes 1048600
  3.8 0.0 copy-start.2
  3.8 1.1 %copy-done.2 = bf16[1,1536,256]{2,1,0:T(8,128)(2,1)S(1)} copy-done((bf16[1,1536,256]{2,1,0:T(8,128)(2,1)S(1)}, bf16[1,1536,256]{2,1,0:T(8,128)(2,1)}, u32[]{:S(2)}) %copy-start.2) | copy-done | bytes 786456
  4.9 0.0 copy-start.3
  4.9 0.9 %copy-done.3 = bf16[1,512,256]{2,1,0:T(8,128)(2,1)S(1)} copy-done((bf16[1,512,256]{2,1,0:T(8,128)(2,1)S(1)}, bf16[1,512,256]{2,1,0:T(8,128)(2,1)}, u32[]{:S(2)}) %copy-start.3) | copy-done | bytes 262168
  5.9 0.0 copy-start.5
  5.9 0.7 %copy-done.5 = bf16[1,512,8]{1,2,0:T(8,128)(2,1)S(1)} copy-done((bf16[1,512,8]{1,2,0:T(8,128)(2,1)S(1)}, bf16[1,512,8]{1,2,0:T(8,128)(2,1)}, u32[]{:S(2)}) %copy-start.5) | copy-done | bytes 8216
  6.6 36.4 %grads.1 = (bf16[512,1024]{1,0:T(8,128)(2,1)S(1)}, bf16[512,256]{1,0:T(8,128)(2,1)S(1)}, bf16[3,512,256]{2,1,0:T(8,128)(2,1)S(1)}) custom-call(s32[1,3]{1,0:T(1,128)S(1)} %copy-done.6, bf16[512,1024]{1,0:T(8,128)(2,1)S(1)} %bitcast.13, bf16[512,1024]{1,0:T(8,128)(2,1)S(1)} %bitcast.14, bf16[8,512]{1,0:T(8,128)(2,1)S(1)} %bitcast.20, ...), custom_call_target="tpu_custom_call" | custom-call | tf_op jit(solution)/shard_map/grads/pallas_call | solution.py:187
  43.0 1.0 %copy.13 = bf16[1,512,1024]{2,1,0:T(8,128)(2,1)} copy(bf16[1,512,1024]{2,1,0:T(8,128)(2,1)S(1)} %bitcast.15) | data formatting | bytes 2097152
  43.9 0.7 %copy.14 = bf16[1,512,256]{2,1,0:T(8,128)(2,1)} copy(bf16[1,512,256]{2,1,0:T(8,128)(2,1)S(1)} %bitcast.18) | data formatting | bytes 524288
  44.7 0.9 %copy.15 = bf16[1,1536,256]{2,1,0:T(8,128)(2,1)} copy(bf16[1,1536,256]{2,1,0:T(8,128)(2,1)S(1)} %bitcast.16) | data formatting | bytes 1572864
Async XLA Ops:
  0.6 0.7 %copy-start.4 = (bf16[1,512,8]{1,2,0:T(8,128)(2,1)S(1)}, bf16[1,512,8]{1,2,0:T(8,128)(2,1)}, u32[]{:S(2)}) copy-start(bf16[1,512,8]{1,2,0:T(8,128)(2,1)} %param.9) | copy-start | bytes 24580
  0.6 0.7 %copy-start.6 = (s32[1,3]{1,0:T(1,128)S(1)}, s32[1,3]{1,0:T(1,128)}, u32[]{:S(2)}) copy-start(s32[1,3]{1,0:T(1,128)} %table.1) | copy-start | bytes 40
  1.3 1.2 %copy-start = (bf16[1,512,1024]{2,1,0:T(8,128)(2,1)S(1)}, bf16[1,512,1024]{2,1,0:T(8,128)(2,1)}, u32[]{:S(2)}) copy-start(bf16[1,512,1024]{2,1,0:T(8,128)(2,1)} %param.7) | copy-start | bytes 3145732
  2.6 1.2 %copy-start.1 = (bf16[1,512,1024]{2,1,0:T(8,128)(2,1)S(1)}, bf16[1,512,1024]{2,1,0:T(8,128)(2,1)}, u32[]{:S(2)}) copy-start(bf16[1,512,1024]{2,1,0:T(8,128)(2,1)} %param.8) | copy-start | bytes 3145732
  3.8 1.1 %copy-start.2 = (bf16[1,1536,256]{2,1,0:T(8,128)(2,1)S(1)}, bf16[1,1536,256]{2,1,0:T(8,128)(2,1)}, u32[]{:S(2)}) copy-start(bf16[1,1536,256]{2,1,0:T(8,128)(2,1)} %param.12) | copy-start | bytes 2359300
  4.9 0.9 %copy-start.3 = (bf16[1,512,256]{2,1,0:T(8,128)(2,1)S(1)}, bf16[1,512,256]{2,1,0:T(8,128)(2,1)}, u32[]{:S(2)}) copy-start(bf16[1,512,256]{2,1,0:T(8,128)(2,1)} %param.11) | copy-start | bytes 786436
  5.9 0.7 %copy-start.5 = (bf16[1,512,8]{1,2,0:T(8,128)(2,1)S(1)}, bf16[1,512,8]{1,2,0:T(8,128)(2,1)}, u32[]{:S(2)}) copy-start(bf16[1,512,8]{1,2,0:T(8,128)(2,1)} %param.10) | copy-start | bytes 24580

commit v2 on v1

--- a/solution.py
+++ b/solution.py
@@ -20,10 +20,10 @@
 
 def kernel(
     slots, heads, table, q_hbm, g_hbm, lt_hbm, off_hbm, own_hbm, pool_hbm,
-    dq_hbm, down_hbm, dpool_hbm,
-    q, g, lt, off, own, pool, staged, arrived, outgoing, returned,
-    dq, dq_low, dk, dv, down, dpool, lt_t, off_t,
-    in_sem, out_sem, ksend, krecv, gsend, grecv,
+    dq_hbm, down_hbm, returned,
+    q, g, lt, off, own, pool, staged, arrived, outgoing,
+    dq, dk, dv, dq_low, down, zeros, lt_t, off_t,
+    in_sem, out_sem, zero_sem, ksend, krecv, gsend, grecv,
 ):
     chunk = staged.shape[1]
     parts = staged.shape[0] // slots
@@ -75,13 +75,18 @@
     def grads_copy(n):
         return remote(outgoing, returned, gsend, grecv, n)
 
+    def zero_copy(n):
+        return pltpu.make_async_copy(zeros, returned.at[n], zero_sem.at[n])
+
     @pl.loop(0, theirs)
     def _(n):
         keys_copy(n).start()
 
+    zeros[...] = jnp.zeros(zeros.shape, zeros.dtype)
+
     @pl.loop(theirs, slots * parts)
     def _(n):
-        returned[n] = jnp.zeros(returned.shape[1:], returned.dtype)
+        zero_copy(n).start()
 
     for copy in ins[1:]:
         copy.wait()
@@ -100,7 +105,7 @@
         weights_low = weights.astype(jnp.bfloat16)
         score_low = grads.astype(jnp.bfloat16)
         return (
-            dot(score_low, key, 0, 0),
+            dot(key, score_low, 0, 0),
             dot(score_low, qh, 1, 0),
             dot(weights_low, gh, 1, 0),
         )
@@ -116,9 +121,9 @@
             )
             dq_t, dk_t, dv_t = tile(own[keys, :head], own[keys, head:], h, first, mask)
             if t == 0:
-                dq[:, cols] = dq_t
+                dq[cols] = dq_t
             else:
-                dq[first:, cols] += dq_t
+                dq[cols, first:] += dq_t
             if h == 0:
                 dk[keys] = dk_t
                 dv[keys] = dv_t
@@ -136,7 +141,7 @@
         for h in range(heads):
             cols = slice(h * head, (h + 1) * head)
             dq_t, dk_t, dv_t = tile(arrived[n, :, :head], arrived[n, :, head:], h, 0, None)
-            dq[:, cols] += dq_t
+            dq[cols] += dq_t
             if h == 0:
                 dk[:chunk] = dk_t
                 dv[:chunk] = dv_t
@@ -147,7 +152,9 @@
         outgoing[n, :, head:] = dv[:chunk].astype(outgoing.dtype)
         grads_copy(n).start()
 
-    dq_low[...] = (dq[...] * scale).astype(dq_low.dtype)
+    for h in range(heads):
+        cols = slice(h * head, (h + 1) * head)
+        dq_low[:, cols] = (dq[cols].T * scale).astype(dq_low.dtype)
     dq_out = pltpu.make_async_copy(dq_low, dq_hbm, out_sem.at[1])
     dq_out.start()
 
@@ -156,22 +163,43 @@
         keys_copy(n).wait_send()
         grads_copy(n).wait_recv()
 
+    @pl.loop(0, mine)
+    def _(n):
+        grads_copy(n).wait_send()
+
+    @pl.loop(theirs, slots * parts)
+    def _(n):
+        zero_copy(n).wait()
+
+    down_out.wait()
+    dq_out.wait()
+
+
+def finish(
+    slots, table, dq, down, returned, dq_hbm, down_hbm, dpool_hbm, dq_low, down_low, pool, isem, osem
+):
+    parts = returned.shape[0] // slots
+    ins, outs = [(dq, dq_low), (down, down_low)], [(dq_low, dq_hbm), (down_low, down_hbm)]
     for slot in range(slots):
         place = jnp.int32(0)
         for position in range(1, slots):
             place = jnp.where(table[0, position] == slot, position, place)
-        for part in range(parts):
-            dpool[slot * parts + part] = returned[place * parts + part]
-    dpool_out = pltpu.make_async_copy(dpool, dpool_hbm, out_sem.at[2])
-    dpool_out.start()
-
-    @pl.loop(0, mine)
-    def _(n):
-        grads_copy(n).wait_send()
-
-    down_out.wait()
-    dq_out.wait()
-    dpool_out.wait()
+        block = pl.ds(slot * parts, parts)
+        ins.append((returned.at[pl.ds(place * parts, parts)], pool.at[block]))
+        outs.append((pool.at[block], dpool_hbm.at[block]))
+    ins = [
+        pltpu.make_async_copy(src, dst, isem.at[n]) for n, (src, dst) in enumerate(ins)
+    ]
+    outs = [
+        pltpu.make_async_copy(src, dst, osem.at[n]) for n, (src, dst) in enumerate(outs)
+    ]
+    for copy in ins:
+        copy.start()
+    for first, second in zip(ins, outs):
+        first.wait()
+        second.start()
+    for copy in outs:
+        copy.wait()
 
 
 def per_device(query, grad_output, log_total, offset, slice_keys, pool_keys, block_table):
@@ -182,17 +210,19 @@
     chunk = rows // PARTS
     pool = pool_keys.reshape(total, chunk, width)
     low = jnp.bfloat16
-    hbm = pl.BlockSpec(memory_space=pl.ANY)
+    smem = pl.BlockSpec(memory_space=pltpu.SMEM)
+    anywhere = pl.BlockSpec(memory_space=pl.ANY)
     block = (total, chunk, width)
-    dq, down, dpool = pl.pallas_call(
+    results = (
+        jax.ShapeDtypeStruct(query.shape[1:], low),
+        jax.ShapeDtypeStruct(slice_keys.shape[1:], low),
+        jax.ShapeDtypeStruct(block, low),
+    )
+    held = pl.pallas_call(
         functools.partial(kernel, slots, heads),
-        out_shape=(
-            jax.ShapeDtypeStruct(query.shape[1:], low),
-            jax.ShapeDtypeStruct(slice_keys.shape[1:], low),
-            jax.ShapeDtypeStruct(block, low),
-        ),
-        in_specs=[pl.BlockSpec(memory_space=pltpu.SMEM)] + [hbm] * 6,
-        out_specs=(hbm, hbm, hbm),
+        out_shape=results,
+        in_specs=[smem] + [anywhere] * 6,
+        out_specs=(anywhere,) * 3,
         scratch_shapes=[
             pltpu.VMEM(query.shape[1:], low),
             pltpu.VMEM(query.shape[1:], low),
@@ -203,27 +233,42 @@
             pltpu.VMEM(block, low),
             pltpu.VMEM(block, low),
             pltpu.VMEM(block, low),
-            pltpu.VMEM(block, low),
-            pltpu.VMEM(query.shape[1:], jnp.float32),
-            pltpu.VMEM(query.shape[1:], low),
+            pltpu.VMEM((query.shape[2], rows), jnp.float32),
             pltpu.VMEM((rows, width // 2), jnp.float32),
             pltpu.VMEM((rows, width // 2), jnp.float32),
+            pltpu.VMEM(query.shape[1:], low),
             pltpu.VMEM((rows, width), low),
-            pltpu.VMEM(block, low),
+            pltpu.VMEM((chunk, width), low),
             pltpu.VMEM((heads, rows), jnp.float32),
             pltpu.VMEM((heads, rows), jnp.float32),
             pltpu.SemaphoreType.DMA((6,)),
-            pltpu.SemaphoreType.DMA((3,)),
+            pltpu.SemaphoreType.DMA((2,)),
+            pltpu.SemaphoreType.DMA((total,)),
             pltpu.SemaphoreType.DMA((total,)),
             pltpu.SemaphoreType.DMA((total,)),
             pltpu.SemaphoreType.DMA((total,)),
             pltpu.SemaphoreType.DMA((total,)),
         ],
         compiler_params=pltpu.CompilerParams(
-            collective_id=0, has_side_effects=True, vmem_limit_bytes=48 * 1024 * 1024
+            collective_id=0, has_side_effects=True, vmem_limit_bytes=56 * 1024 * 1024
         ),
         name="grads",
     )(block_table, query[0], grad_output[0], log_total[0].T, offset[0].T, slice_keys[0], pool)
+    dq, down, dpool = pl.pallas_call(
+        functools.partial(finish, slots),
+        out_shape=results,
+        in_specs=[smem] + [anywhere] * 3,
+        out_specs=(anywhere,) * 3,
+        scratch_shapes=[
+            pltpu.VMEM(query.shape[1:], low),
+            pltpu.VMEM((rows, width), low),
+            pltpu.VMEM(block, low),
+            pltpu.SemaphoreType.DMA((2 + slots,)),
+            pltpu.SemaphoreType.DMA((2 + slots,)),
+        ],
+        compiler_params=pltpu.CompilerParams(vmem_limit_bytes=56 * 1024 * 1024),
+        name="finish",
+    )(block_table, *held)
     return dq[None], down[None], dpool.reshape(pool_keys.shape)
 
 

time: 45.9 us -> 39.9 us (0.87)
  local copies, waits for them, and re-layouts: 8.47 us -> 0 us
  Pallas kernels: 36.4 us -> 39 us
    unnamed x17 -> x0, local copies, waits for them, and re-layouts: 8.47 us -> none
    pallas_call x1 -> x2, Pallas kernels: 36.4 us -> 39 us  [the longest x1 35.7 us: per_device(): pl.pallas_call(functools.partial(kernel, slots, heads), out_shape=results...]
where the time goes in v2:
time: 39.9 us; the launch traced here: 39.7 us
  Pallas kernels  39 us (98%)
  between operations  0.64 us (2%)
    pallas_call x1, Pallas kernels, per_device(): pl.pallas_call(functools.partial(kernel, slots, heads), out_shape=results...  35.7 us
    pallas_call x1, Pallas kernels, per_device(): pl.pallas_call(functools.partial(finish, slots), out_shape=results, in_sp...  3.28 us

profile of v2, /device:TPU:0, one launch (start us, length us, event | category | flops | bytes accessed | tf_op | source)
XLA Modules:
  0.0 39.7 jit_solution(1145057996853281564)
XLA Ops:
  0.6 35.7 %grads.1 = (bf16[512,1024]{1,0:T(8,128)(2,1)}, bf16[512,256]{1,0:T(8,128)(2,1)}, bf16[3,512,256]{2,1,0:T(8,128)(2,1)}) custom-call(s32[1,3]{1,0:T(1,128)} %table.3, bf16[512,1024]{1,0:T(8,128)(2,1)} %bitcast.13, bf16[512,1024]{1,0:T(8,128)(2,1)} %bitcast.14, bf16[8,512]{1,0:T(8,128)(2,1)} %bitcast.17, bf16[8,512]{1,0:T(8,128)(2,1)} %bitcast.18, ...), custom_call_target="tpu_custom_call" | custom-call | tf_op jit(solution)/shard_map/grads/pallas_call | solution.py:221
  36.4 3.3 %finish.1 = (bf16[512,1024]{1,0:T(8,128)(2,1)}, bf16[512,256]{1,0:T(8,128)(2,1)}, bf16[3,512,256]{2,1,0:T(8,128)(2,1)}) custom-call(s32[1,3]{1,0:T(1,128)} %table.3, bf16[512,1024]{1,0:T(8,128)(2,1)} %get-tuple-element.9.dq, bf16[512,256]{1,0:T(8,128)(2,1)} %get-tuple-element.10.down, bf16[3,512,256]{2,1,0:T(8,128)(2,1)} %get-tuple-element.11.returned), custom_call_target="tpu_custom_call" | custom-call | tf_op jit(solution)/shard_map/finish/pallas_call | solution.py:257
